TPU v7x, 32 devices: a whole 2x2x4 slice. The times are simulated.
32 devices in a mesh: section: 4 (over x, core), sub: 2 (over y), rng: 4 (over z).
Axes of the slice: x: 2, y: 2, z: 4, core: 2. Of those that a mesh axis runs over, the one named last changes fastest.
Arguments:
- echoes: bfloat16 [2, 2, 24, 16384], P(None, 'sub', 'section', 'rng'), may hold values from -6 to 6
- chirp: bfloat16 [2, 2048], replicated, may hold values from -0.25 to 0.25
- steer: bfloat16 [2, 2, 128, 24], P(None, 'sub'), may hold values from -2 to 2
- pulse_order: int32 [2, 24], P('sub'), may hold values from 0 to 23, each once within a row
- band_coef: bfloat16 [5, 2, 2, 2, 128, 16], P(None, 'sub'), may hold values from -2.5 to 2.5
- band_start: int32 [5, 2, 2, 128], P(None, 'sub'), may hold values from 0 to 112
- band_width: int32 [5, 2, 2, 128], P(None, 'sub'), may hold values from 1 to 16
Outputs:
- image: bfloat16 [2, 256, 4, 4096], P(None, 'sub', 'rng', 'section')
Inputs may be any that keep to these rules, and one draw needn't show every extreme that they name: `pulse_order`: each row is a permutation of the 24 aperture positions.
All inputs are finite; a program needn't handle non-finite values.
Results may differ from a plain program's by a relative error of at most 0.0085.
Values may be sent and summed in bfloat16 or wider, within the bound.
No kernel may reach another device: no remote copies, remote signals or barrier semaphores. Data moves between devices by JAX's collectives and lax.ppermute only.
A program may use at most 64 MiB of HBM per device.

v0:
```python
import functools

import jax
import jax.numpy as jnp
from jax import lax
from jax.experimental import pallas as pl
from jax.experimental.pallas import tpu as pltpu
from jax.sharding import PartitionSpec as P

LANE = 128
SUBL = 8
F32 = jnp.float32
BF16 = jnp.bfloat16


def ceil_to(value, unit):
    return -(-value // unit) * unit


def prepare_kernel(*refs, sections, group):
    sources, (echo_out, chirp_out, pack_ref), scratch = refs[:7], refs[7:10], refs[10:]
    coef_ref, start_ref, width_ref, steer_ref, order_ref, starts, sems = scratch
    targets = (coef_ref, start_ref, width_ref, steer_ref, order_ref, chirp_out, echo_out)
    loads = [
        pltpu.make_async_copy(source, target, sems.at[i])
        for i, (source, target) in enumerate(zip(sources, targets))
    ]
    for load in loads:
        load.start()
    for load in loads:
        load.wait()
    levels, _, sides, parts, taps, beams = coef_ref.shape
    tap = lax.broadcasted_iota(jnp.int32, (taps, beams), 0)
    row = 0
    for level in range(levels):
        for side in range(sides):
            used = tap < width_ref[level, 0, side : side + 1, :]
            for part in range(parts):
                entries = coef_ref[level, 0, side, part].astype(F32)
                pack_ref[row : row + taps] = jnp.where(used, entries, 0.0).astype(BF16)
                row += taps
    pulses = order_ref.shape[1]
    each = pulses // sections
    position = lax.broadcasted_iota(jnp.int32, (pulses, pulses), 0)
    hit = (position == order_ref[0:1, :]).astype(F32)
    slot = lax.broadcasted_iota(jnp.int32, (sections * group, pulses), 0)
    pulse = lax.broadcasted_iota(jnp.int32, (sections * group, pulses), 1)
    place = jnp.zeros((sections * group, pulses), F32)
    for s in range(sections):
        inside = (pulse >= s * each) & (pulse < (s + 1) * each)
        place = jnp.where(inside & (slot - s * group == pulse - s * each), 1.0, place)
    pick = lax.dot_general(
        place.astype(BF16), hit.astype(BF16), (((1,), (1,)), ((), ())), preferred_element_type=F32
    )
    for part in range(parts):
        chosen = jnp.dot(pick.astype(BF16), steer_ref[part, 0], preferred_element_type=F32)
        pack_ref[row : row + sections * group] = chosen.astype(BF16)
        row += sections * group
    starts[...] = jnp.zeros_like(starts)
    for level in range(levels):
        starts[sides * level : sides * level + sides] = start_ref[level, 0].astype(F32)
    pack_ref[row : row + starts.shape[0]] = starts[...].astype(BF16)


def pack_rows(levels, sides, parts, taps, sections, group):
    return levels * sides * parts * taps + parts * sections * group + ceil_to(levels * sides, 16)


def prepare(echo, chirp, coef, start, width, steer, order, sections, group):
    levels, _, sides, parts, taps, beams = coef.shape
    sources = (coef, start, width, steer, order, chirp, echo)
    return pl.pallas_call(
        functools.partial(prepare_kernel, sections=sections, group=group),
        out_shape=(
            jax.ShapeDtypeStruct(echo.shape, BF16),
            jax.ShapeDtypeStruct(chirp.shape, BF16),
            jax.ShapeDtypeStruct((pack_rows(levels, sides, parts, taps, sections, group), beams), BF16),
        ),
        in_specs=[pl.BlockSpec(memory_space=pl.ANY)] * len(sources),
        scratch_shapes=[pltpu.VMEM(x.shape, x.dtype) for x in sources[:5]]
        + [pltpu.VMEM((ceil_to(levels * sides, 16), beams), F32), pltpu.SemaphoreType.DMA((len(sources),))],
        name="prepare",
    )(*sources)


def split_two(value):
    high = value.astype(BF16)
    return high, (value - high.astype(F32)).astype(BF16)


def operator_kernel(index_ref, own_ref, partner_ref, out_ref, weights, *, dims, sections, group):
    levels, sides, parts, taps, beams = dims
    width = sections * group
    refs = (own_ref, partner_ref)
    weight_row = levels * sides * parts * taps
    start_row = weight_row + parts * width

    def band(ref, level, side):
        first = ((level * sides + side) * parts) * taps
        tables = [ref[first + p * taps : first + (p + 1) * taps].astype(F32) for p in range(parts)]
        start = ref[start_row : start_row + ceil_to(levels * sides, 16)].astype(F32)
        start = start[level * sides + side : level * sides + side + 1].astype(jnp.int32)
        found = [[], []]
        for c in range(0, beams, SUBL):
            column = lax.broadcasted_iota(jnp.int32, (SUBL, beams), 0) + c
            offset = column - start
            spot = offset & (SUBL - 1)
            for p in range(parts):
                value = jnp.zeros((SUBL, beams), F32)
                for t in range(0, taps, SUBL):
                    got = jnp.take_along_axis(
                        tables[p][t : t + SUBL], spot, axis=0, mode="promise_in_bounds"
                    )
                    value = jnp.where((offset >= t) & (offset < t + SUBL), got, value)
                found[p].append(value)
        return [jnp.concatenate(f, axis=0) for f in found]

    def complex_operand(real, imag):
        top = jnp.concatenate([real, imag], axis=1)
        low = jnp.concatenate([-imag, real], axis=1)
        return jnp.concatenate([top, low], axis=0).astype(BF16)

    section = index_ref[0]
    images = []
    for a in range(2):
        for p in range(parts):
            weights[...] = refs[a][weight_row + p * width : weight_row + (p + 1) * width].astype(F32)
            rows = []
            for j in range(sections):
                at = pl.multiple_of((section ^ j) * group, group)
                rows.append(weights[pl.ds(at, group)])
            images.append(jnp.concatenate(rows, axis=0))
    zero = jnp.zeros((width, 2 * beams), F32)
    own = jnp.concatenate([jnp.concatenate(images[0:2], axis=1), zero], axis=0)
    partner = jnp.concatenate([zero, jnp.concatenate(images[2:4], axis=1)], axis=0)
    for level in range(levels):
        own_high, own_low = split_two(own)
        partner_high, partner_low = split_two(partner)
        own_rows = jnp.concatenate([own_high, own_low], axis=0)
        partner_rows = jnp.concatenate([partner_high, partner_low], axis=0)

        def merged(ref, mine, other):
            product = jnp.dot(
                mine, complex_operand(*band(ref, level, 0)), preferred_element_type=F32
            ) + jnp.dot(other, complex_operand(*band(ref, level, 1)), preferred_element_type=F32)
            return product[: 2 * width] + product[2 * width :]

        following = merged(own_ref, own_rows, partner_rows)
        if level < levels - 1:
            partner = merged(partner_ref, partner_rows, own_rows)
        own = following
    blocks = []
    for j in range(2 * sections):
        real = own[j * group : (j + 1) * group, :beams]
        imag = own[j * group : (j + 1) * group, beams:]
        blocks.append(jnp.concatenate([real, imag], axis=1))
        blocks.append(jnp.concatenate([-imag, real], axis=1))
    whole = jnp.concatenate(blocks, axis=0).T
    high, low = split_two(whole)
    out_ref[...] = jnp.concatenate([high, low], axis=1)


def fold_operator(index, own, partner, dims, sections, group):
    beams = dims[-1]
    width = sections * group
    return pl.pallas_call(
        functools.partial(operator_kernel, dims=dims, sections=sections, group=group),
        out_shape=jax.ShapeDtypeStruct((2 * beams, 8 * width), BF16),
        in_specs=[
            pl.BlockSpec(memory_space=pltpu.SMEM),
            pl.BlockSpec(memory_space=pltpu.VMEM),
            pl.BlockSpec(memory_space=pltpu.VMEM),
        ],
        scratch_shapes=[pltpu.VMEM((width, beams), F32)],
        compiler_params=pltpu.CompilerParams(vmem_limit_bytes=16 * 1024 * 1024),
        name="fold_operator",
    )(index, own, partner)


def correlate(rows, even, odd, table, blocks, extra, group):
    total = blocks + extra
    held = [
        jnp.concatenate(
            [rows[:group, b * LANE : (b + 1) * LANE], rows[group:, b * LANE : (b + 1) * LANE]], axis=1
        )
        for b in range(total)
    ]
    for b in range(0, total, 2):
        even[b * group : (b + 2) * group] = jnp.concatenate(held[b : b + 2], axis=0).astype(BF16)
    for b in range(1, total - 1, 2):
        odd[(b - 1) * group : (b + 1) * group] = jnp.concatenate(held[b : b + 2], axis=0).astype(BF16)
    window = blocks * group
    pieces = []
    for lag in range(extra + 1):
        source, at = (even, lag) if lag % 2 == 0 else (odd, lag - 1)
        pieces.append(source[at * group : at * group + window])
    return jnp.dot(jnp.concatenate(pieces, axis=1), table[...], preferred_element_type=F32)


def as_chunk(done, s, chunk, group):
    return jnp.concatenate(
        [
            jnp.concatenate(
                [
                    done[(s * chunk + b) * group : (s * chunk + b + 1) * group, c * LANE : (c + 1) * LANE]
                    for b in range(chunk)
                ],
                axis=1,
            )
            for c in range(2)
        ],
        axis=0,
    ).astype(BF16)


def begin_kernel(echo_ref, chirp_ref, out_ref, late_ref, table, rows, even, odd, *, group):
    pulses, _, length = echo_ref.shape
    extra = chirp_ref.shape[1] // LANE
    reverse = LANE - 1 - lax.broadcasted_iota(jnp.int32, (2, LANE), 1)
    below = lax.broadcasted_iota(jnp.int32, (LANE, LANE), 1) <= lax.broadcasted_iota(
        jnp.int32, (LANE, LANE), 0
    )
    before = [jnp.zeros((LANE, LANE), F32)] * 2
    for lag in range(extra + 1):
        if lag < extra:
            piece = chirp_ref[:, lag * LANE : (lag + 1) * LANE].astype(F32)
            piece = jnp.take_along_axis(piece, reverse, axis=1, mode="promise_in_bounds")
            turned = [
                pltpu.roll(
                    jnp.broadcast_to(piece[c : c + 1], (LANE, LANE)), 1, 1, stride=1, stride_axis=0
                )
                for c in range(2)
            ]
        else:
            turned = [jnp.zeros((LANE, LANE), F32)] * 2
        real, imag = [jnp.where(below, turned[c], before[c]) for c in range(2)]
        before = turned
        at = lag * 2 * LANE
        table[at : at + LANE, :LANE] = real.astype(BF16)
        table[at : at + LANE, LANE:] = (-imag).astype(BF16)
        table[at + LANE : at + 2 * LANE, :LANE] = imag.astype(BF16)
        table[at + LANE : at + 2 * LANE, LANE:] = real.astype(BF16)
    rows[...] = jnp.zeros_like(rows)
    for p in range(pulses):
        near = echo_ref[p].astype(F32)
        for c in range(2):
            rows[c * group + p : c * group + p + 1, :] = near[c : c + 1]
    late_ref[...] = rows[:, length - late_ref.shape[1] :]
    done = correlate(rows, even, odd, table, length // LANE - extra, extra, group)
    for s in range(out_ref.shape[0]):
        out_ref[s] = as_chunk(done, s, out_ref.shape[2] // LANE, group)


def finish_kernel(index_ref, early_ref, late_ref, halo_ref, table, out_ref, rows, even, odd, *, group):
    section, has_next = index_ref[0], index_ref[1] != 0
    pulses = halo_ref.shape[0]
    span = late_ref.shape[1]
    extra = even.shape[0] // group - span // LANE
    taps = extra * LANE
    rows[:, :span] = late_ref[...]
    rows[:, span:] = jnp.zeros((2 * group, taps), F32)
    for p in range(pulses):
        far = halo_ref[p, :, :taps].astype(F32)
        far = jnp.where(has_next, far, 0.0)
        for c in range(2):
            rows[c * group + p : c * group + p + 1, span:] = far[c : c + 1]
    done = correlate(rows, even, odd, table, span // LANE, extra, group)
    ready = early_ref.shape[0]
    for s in range(ready):
        out_ref[section ^ s] = early_ref[s]
    for s in range(ready, out_ref.shape[0]):
        out_ref[section ^ s] = as_chunk(done, s - ready, out_ref.shape[2] // LANE, group)


def row_scratch(blocks, group):
    return [
        pltpu.VMEM((2 * group, blocks * LANE), F32),
        pltpu.VMEM((blocks * group, 2 * LANE), BF16),
        pltpu.VMEM((blocks * group, 2 * LANE), BF16),
    ]


def begin_compression(echo, chirp, sections, group):
    _, _, length = echo.shape
    taps = chirp.shape[1]
    extra = taps // LANE
    chunk = length // sections
    early = (length - taps) // chunk
    return pl.pallas_call(
        functools.partial(begin_kernel, group=group),
        out_shape=(
            jax.ShapeDtypeStruct((early, 2 * group, chunk), BF16),
            jax.ShapeDtypeStruct((2 * group, length - early * chunk), F32),
            jax.ShapeDtypeStruct(((extra + 1) * 2 * LANE, 2 * LANE), BF16),
        ),
        scratch_shapes=row_scratch(length // LANE, group),
        compiler_params=pltpu.CompilerParams(vmem_limit_bytes=24 * 1024 * 1024),
        name="begin_compression",
    )(echo, chirp)


def finish_compression(index, early, late, halo, table, sections, group):
    _, height, chunk = early.shape
    blocks = late.shape[1] // LANE + table.shape[0] // (2 * LANE) - 1
    return pl.pallas_call(
        functools.partial(finish_kernel, group=group),
        out_shape=jax.ShapeDtypeStruct((sections, height, chunk), BF16),
        in_specs=[pl.BlockSpec(memory_space=pltpu.SMEM)] + [pl.BlockSpec(memory_space=pltpu.VMEM)] * 4,
        scratch_shapes=row_scratch(blocks, group),
        compiler_params=pltpu.CompilerParams(vmem_limit_bytes=24 * 1024 * 1024),
        name="finish_compression",
    )(index, early, late, halo, table)


def image_kernel(operator_ref, *refs):
    chunks, (out_ref, parts, sems) = refs[:-3], refs[-3:]
    count, _, tile = parts.shape
    operator = operator_ref[...]
    copies = []
    for i in range(count):
        pulses = [chunk[:, i * tile : (i + 1) * tile] for chunk in chunks]
        result = jnp.dot(operator, jnp.concatenate(pulses + pulses, axis=0), preferred_element_type=F32)
        parts[i] = result.astype(BF16)
        copy = pltpu.make_async_copy(parts.at[i], out_ref.at[:, i * tile : (i + 1) * tile], sems.at[i])
        copy.start()
        copies.append(copy)
    for copy in copies:
        copy.wait()


def form_image(operator, chunks):
    height, width = operator.shape[0], chunks[0].shape[1]
    tile = 256 if width % 256 == 0 else width
    return pl.pallas_call(
        image_kernel,
        out_shape=jax.ShapeDtypeStruct((height, width), BF16),
        in_specs=[pl.BlockSpec(memory_space=pltpu.VMEM)] * (1 + len(chunks)),
        out_specs=pl.BlockSpec(memory_space=pl.ANY),
        scratch_shapes=[
            pltpu.VMEM((width // tile, height, tile), BF16),
            pltpu.SemaphoreType.DMA((width // tile,)),
        ],
        compiler_params=pltpu.CompilerParams(vmem_limit_bytes=16 * 1024 * 1024),
        name="form_image",
    )(operator, *chunks)


def swap(value, axis, by):
    count = lax.axis_size(axis)
    return lax.ppermute(value, axis, [(i, i ^ by) for i in range(count)])


def swap_both(value, by_section, by_sub):
    sections, subs = lax.axis_size("section"), lax.axis_size("sub")
    pairs = [
        (s * subs + a, (s ^ by_section) * subs + (a ^ by_sub)) for s in range(sections) for a in range(subs)
    ]
    return lax.ppermute(value, ("section", "sub"), pairs)


def from_next(value, axis):
    count = lax.axis_size(axis)
    return lax.ppermute(value, axis, [(i, (i - 1) % count) for i in range(count)])


def on_device(echoes, chirp, steer, pulse_order, band_coef, band_start, band_width):
    sections, subs = lax.axis_size("section"), lax.axis_size("sub")
    pulses_each = echoes.shape[2]
    group = ceil_to(pulses_each, SUBL)
    coef = jnp.swapaxes(band_coef, 4, 5)
    weights = jnp.swapaxes(steer, 2, 3)
    levels, _, sides, parts, taps, beams = coef.shape
    dims = (levels, sides, parts, taps, beams)

    section = lax.axis_index("section").astype(jnp.int32)
    has_next = (lax.axis_index("rng") < lax.axis_size("rng") - 1).astype(jnp.int32)
    index = jnp.stack([section, has_next])
    echo = jnp.transpose(echoes[:, 0], (1, 0, 2))
    halo = from_next(echo, "rng")
    echo, chirp, packed = prepare(
        echo, chirp, coef, band_start, band_width, weights, pulse_order, sections, group
    )
    packed_partner = swap(packed, "sub", 1) if subs == 2 else packed
    early, late, table = begin_compression(echo, chirp, sections, group)
    halo, packed_partner = lax.optimization_barrier((halo, packed_partner))
    compressed = finish_compression(index, early, late, halo, table, sections, group)
    chunks = [compressed[0]] + [swap(compressed[j], "section", j) for j in range(1, sections)]
    if subs != 2:
        return merge_images(section, chunks, packed, dims, sections, group)
    chunks += [swap_both(compressed[j], j, 1) for j in range(sections)]
    operator = fold_operator(index, packed, packed_partner, dims, sections, group)
    image = form_image(operator, chunks)
    return image.reshape(2, beams, 1, image.shape[1])


def merge_images(section, chunks, packed, dims, sections, group):
    levels, sides, parts, taps, beams = dims
    width = sections * group
    first = levels * sides * parts * taps
    table = packed[first : first + parts * width].reshape(parts, sections, group, beams)
    table = jnp.take(table, section ^ jnp.arange(sections), axis=1)
    real, imag = table[0], table[1]
    rows = jnp.concatenate(
        [jnp.concatenate([real, -imag], axis=1), jnp.concatenate([imag, real], axis=1)], axis=2
    ).reshape(sections * 2 * group, 2 * beams)
    image = lax.dot_general(
        rows, jnp.concatenate(chunks, axis=0), (((0,), (0,)), ((), ())), preferred_element_type=F32
    ).astype(BF16)
    starts = packed[first + parts * width :].astype(jnp.int32)
    column = jnp.arange(beams, dtype=jnp.int32)
    bits = lax.axis_size("sub").bit_length() - 1
    for level in range(levels):
        partner = swap(image, "sub", 1 << (level % bits))
        operands = []
        for side in range(sides):
            at = (level * sides + side) * parts * taps
            coef = packed[at : at + parts * taps].reshape(parts, taps, beams)
            offset = column[:, None] - starts[level * sides + side][None, :]
            hits = (offset[None] == jnp.arange(taps, dtype=jnp.int32)[:, None, None]).astype(BF16)
            operands.append(jnp.einsum("ptq,tcq->pqc", coef, hits, preferred_element_type=F32).astype(BF16))
        top = jnp.concatenate([operands[0][0], -operands[0][1], operands[1][0], -operands[1][1]], axis=1)
        low = jnp.concatenate([operands[0][1], operands[0][0], operands[1][1], operands[1][0]], axis=1)
        image = jnp.dot(
            jnp.concatenate([top, low], axis=0),
            jnp.concatenate([image, partner], axis=0),
            preferred_element_type=F32,
        ).astype(BF16)
    return image.reshape(2, beams, 1, image.shape[1])


def solution(mesh):
    return jax.shard_map(
        on_device,
        mesh=mesh,
        in_specs=(
            P(None, "sub", "section", "rng"),
            P(),
            P(None, "sub", None, None),
            P("sub", None),
            P(None, "sub", None, None, None, None),
            P(None, "sub", None, None),
            P(None, "sub", None, None),
        ),
        out_specs=P(None, "sub", "rng", "section"),
        check_vma=False,
    )
```

profile of v0, /device:TPU:0, one launch (start us, length us, event | category | flops | bytes accessed | tf_op | source)
XLA Modules:
  0.0 24.4 jit_solution(792357279936286326)
XLA Ops:
  0.0 5.0 %collective-permute-start = (bf16[6,2,4096]{2,1,0:T(2,128)(2,1)}, bf16[6,2,4096]{2,1,0:T(2,128)(2,1)S(1)}, u32[]{:S(2)}, u32[]{:S(2)}) collective-permute-start(bf16[6,2,4096]{2,1,0:T(2,128)(2,1)} %bitcast.18), channel_id=1, source_target_pairs={{0,3},{1,0},{2,1},{3,2},{4,7},{5,4},{6,5},{7,6},{8,11},{9,8},{10,9... | collective-permute-start | bytes 294920 | tf_op jit(solution)/shard_map/ppermute | solution.py:363
  5.0 2.0 %prepare.1 = (bf16[6,2,4096]{2,1,0:T(2,128)(2,1)}, bf16[2,2048]{1,0:T(2,128)(2,1)}, bf16[400,128]{1,0:T(8,128)(2,1)}) custom-call(bf16[5,1,2,2,16,128]{5,4,3,2,1,0:T(8,128)(2,1)} %bitcast.20, s32[5,1,2,128]{3,2,1,0:T(2,128)} %refs_1_.1, s32[5,1,2,128]{3,2,1,0:T(2,128)} %refs_2_.1, bf16[2,1,24,128]{3,2,1,0:T(8,128)(2,1)} %bitcast.21, s32[1,24]{1,0:T(1,128)} %refs_4_.1, ...), custom_call_target="tpu_custom_call" | custom-call | tf_op jit(solution)/shard_map/prepare/pallas_call | solution.py:72
  7.0 0.0 copy-start
  7.1 1.6 %collective-permute-start.1 = (bf16[400,128]{1,0:T(8,128)(2,1)}, bf16[400,128]{1,0:T(8,128)(2,1)S(1)}, u32[]{:S(2)}, u32[]{:S(2)}) collective-permute-start(bf16[400,128]{1,0:T(8,128)(2,1)} %get-tuple-element.13.own_ref), channel_id=1, source_target_pairs={{0,4},{4,0},{1,5},{5,1},{2,6},{6,2},{3,7},{7,3},{8,12},{12,8},{9,1... | collective-permute-start | bytes 307208 | tf_op jit(solution)/shard_map/ppermute | solution.py:350
  8.6 0.0 copy-start.1
  8.6 0.9 %copy-done.1 = bf16[6,2,4096]{2,1,0:T(2,128)(2,1)S(1)} copy-done((bf16[6,2,4096]{2,1,0:T(2,128)(2,1)S(1)}, bf16[6,2,4096]{2,1,0:T(2,128)(2,1)}, u32[]{:S(2)}) %copy-start.1) | copy-done | bytes 98328
  9.5 0.0 copy-start.2
  9.5 0.7 %copy-done.2 = bf16[2,2048]{1,0:T(2,128)(2,1)S(1)} copy-done((bf16[2,2048]{1,0:T(2,128)(2,1)S(1)}, bf16[2,2048]{1,0:T(2,128)(2,1)}, u32[]{:S(2)}) %copy-start.2) | copy-done | bytes 8216
  10.2 1.0 %begin_compression.1 = (bf16[2,16,1024]{2,1,0:T(8,128)(2,1)S(1)}, f32[16,2048]{1,0:T(8,128)S(1)}, bf16[4352,256]{1,0:T(8,128)(2,1)S(1)}) custom-call(bf16[6,2,4096]{2,1,0:T(2,128)(2,1)S(1)} %copy-done.1, bf16[2,2048]{1,0:T(2,128)(2,1)S(1)} %copy-done.2), custom_call_target="tpu_custom_call" | custom-call | tf_op jit(solution)/shard_map/begin_compression/pallas_call | solution.py:289
  11.3 0.1 pad_add_fusion.index_ref
  11.3 0.0 collective-permute-done.halo_ref
  11.4 0.6 %collective-permute-done.1.partner_ref = bf16[400,128]{1,0:T(8,128)(2,1)S(1)} collective-permute-done((bf16[400,128]{1,0:T(8,128)(2,1)}, bf16[400,128]{1,0:T(8,128)(2,1)S(1)}, u32[]{:S(2)}, u32[]{:S(2)}) %collective-permute-start.1) | collective-permute-done | bytes 102432 | tf_op jit(solution)/shard_map/ppermute | solution.py:350
  12.0 1.0 %finish_compression.1 = bf16[4,16,1024]{2,1,0:T(8,128)(2,1)S(1)} custom-call(s32[2]{0:T(128)S(1)} %pad_add_fusion.index_ref, bf16[2,16,1024]{2,1,0:T(8,128)(2,1)S(1)} %get-tuple-element.17.early_ref, f32[16,2048]{1,0:T(8,128)S(1)} %get-tuple-element.18.late_ref, bf16[6,2,4096]{2,1,0:T(2,128)(2,1)S(1)} %collective-permute-done.halo_ref, ...), custom_call_target="tpu_custom_call" | custom-call | tf_op jit(solution)/shard_map/finish_compression/pallas_call | solution.py:305
  13.0 0.5 %collective-permute-start.8 = (bf16[16,1024]{1,0:T(8,128)(2,1)S(1)}, bf16[16,1024]{1,0:T(8,128)(2,1)S(1)}, u32[]{:S(2)}, u32[]{:S(2)}) collective-permute-start(bf16[16,1024]{1,0:T(8,128)(2,1)S(1)} %get-tuple-element.21), channel_id=1, source_target_pairs={{0,28},{4,24},{8,20},{12,16},{16,12},{20,8},{24,4},{28,0},{1,29},{... | collective-permute-start | bytes 98312 | tf_op jit(solution)/shard_map/ppermute | solution.py:358
  13.5 2.2 %collective-permute-start.4 = (bf16[16,1024]{1,0:T(8,128)(2,1)S(1)}, bf16[16,1024]{1,0:T(8,128)(2,1)S(1)}, u32[]{:S(2)}, u32[]{:S(2)}) collective-permute-start(bf16[16,1024]{1,0:T(8,128)(2,1)S(1)} %get-tuple-element.21), channel_id=1, source_target_pairs={{0,24},{8,16},{16,8},{24,0},{1,25},{9,17},{17,9},{25,1},{2,26},{10... | collective-permute-start | bytes 98312 | tf_op jit(solution)/shard_map/ppermute | solution.py:350
  15.8 1.4 %collective-permute-start.7 = (bf16[16,1024]{1,0:T(8,128)(2,1)S(1)}, bf16[16,1024]{1,0:T(8,128)(2,1)S(1)}, u32[]{:S(2)}, u32[]{:S(2)}) collective-permute-start(bf16[16,1024]{1,0:T(8,128)(2,1)S(1)} %get-tuple-element.22), channel_id=1, source_target_pairs={{0,20},{4,16},{8,28},{12,24},{16,4},{20,0},{24,12},{28,8},{1,21},{... | collective-permute-start | bytes 98312 | tf_op jit(solution)/shard_map/ppermute | solution.py:358
  17.2 0.5 %collective-permute-start.3 = (bf16[16,1024]{1,0:T(8,128)(2,1)S(1)}, bf16[16,1024]{1,0:T(8,128)(2,1)S(1)}, u32[]{:S(2)}, u32[]{:S(2)}) collective-permute-start(bf16[16,1024]{1,0:T(8,128)(2,1)S(1)} %get-tuple-element.22), channel_id=1, source_target_pairs={{0,16},{8,24},{16,0},{24,8},{1,17},{9,25},{17,1},{25,9},{2,18},{10... | collective-permute-start | bytes 98312 | tf_op jit(solution)/shard_map/ppermute | solution.py:350
  17.8 0.4 %collective-permute-start.6 = (bf16[16,1024]{1,0:T(8,128)(2,1)S(1)}, bf16[16,1024]{1,0:T(8,128)(2,1)S(1)}, u32[]{:S(2)}, u32[]{:S(2)}) collective-permute-start(bf16[16,1024]{1,0:T(8,128)(2,1)S(1)} %get-tuple-element.23), channel_id=1, source_target_pairs={{0,12},{4,8},{8,4},{12,0},{16,28},{20,24},{24,20},{28,16},{1,13},{... | collective-permute-start | bytes 98312 | tf_op jit(solution)/shard_map/ppermute | solution.py:358
  18.2 0.0 collective-permute-done.8.refs_7_
  18.2 1.2 %collective-permute-start.2 = (bf16[16,1024]{1,0:T(8,128)(2,1)S(1)}, bf16[16,1024]{1,0:T(8,128)(2,1)S(1)}, u32[]{:S(2)}, u32[]{:S(2)}) collective-permute-start(bf16[16,1024]{1,0:T(8,128)(2,1)S(1)} %get-tuple-element.23), channel_id=1, source_target_pairs={{0,8},{8,0},{16,24},{24,16},{1,9},{9,1},{17,25},{25,17},{2,10},{10... | collective-permute-start | bytes 98312 | tf_op jit(solution)/shard_map/ppermute | solution.py:350
  19.4 0.0 collective-permute-done.4.refs_3_
  19.4 0.5 %collective-permute-start.5 = (bf16[16,1024]{1,0:T(8,128)(2,1)S(1)}, bf16[16,1024]{1,0:T(8,128)(2,1)S(1)}, u32[]{:S(2)}, u32[]{:S(2)}) collective-permute-start(bf16[16,1024]{1,0:T(8,128)(2,1)S(1)} %get-tuple-element.24.refs_0_), channel_id=1, source_target_pairs={{0,4},{4,0},{8,12},{12,8},{16,20},{20,16},{24,28},{28,24},{1,5},{5... | collective-permute-start | bytes 98312 | tf_op jit(solution)/shard_map/ppermute | solution.py:358
  19.9 0.0 copy-done
  19.9 1.8 %fold_operator.1.operator_ref = bf16[256,256]{1,0:T(8,128)(2,1)S(1)} custom-call(s32[2]{0:T(128)S(1)} %pad_add_fusion.index_ref, bf16[400,128]{1,0:T(8,128)(2,1)S(1)} %copy-done, bf16[400,128]{1,0:T(8,128)(2,1)S(1)} %collective-permute-done.1.partner_ref), custom_call_target="tpu_custom_call" | custom-call | tf_op jit(solution)/shard_map/fold_operator/pallas_call | solution.py:166
  21.7 0.0 collective-permute-done.7.refs_6_
  21.8 0.0 collective-permute-done.3.refs_2_
  21.8 0.0 collective-permute-done.6.refs_5_
  21.8 0.0 collective-permute-done.2.refs_1_
  21.8 1.5 %collective-permute-done.5.refs_4_ = bf16[16,1024]{1,0:T(8,128)(2,1)S(1)} collective-permute-done((bf16[16,1024]{1,0:T(8,128)(2,1)S(1)}, bf16[16,1024]{1,0:T(8,128)(2,1)S(1)}, u32[]{:S(2)}, u32[]{:S(2)}) %collective-permute-start.5) | collective-permute-done | bytes 32800 | tf_op jit(solution)/shard_map/ppermute | solution.py:358
  23.3 1.1 %form_image.1 = bf16[256,1024]{1,0:T(8,128)(2,1)} custom-call(bf16[256,256]{1,0:T(8,128)(2,1)S(1)} %fold_operator.1.operator_ref, bf16[16,1024]{1,0:T(8,128)(2,1)S(1)} %get-tuple-element.24.refs_0_, bf16[16,1024]{1,0:T(8,128)(2,1)S(1)} %collective-permute-done.2.refs_1_, bf16[16,1024]{1,0:T(8,128)(2,1)S(1)} %collective-permute-done.3.refs_2_, ...), custom_call_target="tpu_custom_call" | custom-call | tf_op jit(solution)/shard_map/form_image/pallas_call | solution.py:334
  (1 shorter events, 0.0 us)
Async XLA Ops:
  0.0 11.4 %collective-permute-start = (bf16[6,2,4096]{2,1,0:T(2,128)(2,1)}, bf16[6,2,4096]{2,1,0:T(2,128)(2,1)S(1)}, u32[]{:S(2)}, u32[]{:S(2)}) collective-permute-start(bf16[6,2,4096]{2,1,0:T(2,128)(2,1)} %bitcast.18), channel_id=1, source_target_pairs={{0,3},{1,0},{2,1},{3,2},{4,7},{5,4},{6,5},{7,6},{8,11},{9,8},{10,9... | collective-permute-start | bytes 294920 | tf_op jit(solution)/shard_map/ppermute | solution.py:363
  7.0 12.9 %copy-start = (bf16[400,128]{1,0:T(8,128)(2,1)S(1)}, bf16[400,128]{1,0:T(8,128)(2,1)}, u32[]{:S(2)}) copy-start(bf16[400,128]{1,0:T(8,128)(2,1)} %get-tuple-element.13.own_ref) | copy-start | bytes 307204
  7.1 4.9 %collective-permute-start.1 = (bf16[400,128]{1,0:T(8,128)(2,1)}, bf16[400,128]{1,0:T(8,128)(2,1)S(1)}, u32[]{:S(2)}, u32[]{:S(2)}) collective-permute-start(bf16[400,128]{1,0:T(8,128)(2,1)} %get-tuple-element.13.own_ref), channel_id=1, source_target_pairs={{0,4},{4,0},{1,5},{5,1},{2,6},{6,2},{3,7},{7,3},{8,12},{12,8},{9,1... | collective-permute-start | bytes 307208 | tf_op jit(solution)/shard_map/ppermute | solution.py:350
  8.6 0.9 %copy-start.1 = (bf16[6,2,4096]{2,1,0:T(2,128)(2,1)S(1)}, bf16[6,2,4096]{2,1,0:T(2,128)(2,1)}, u32[]{:S(2)}) copy-start(bf16[6,2,4096]{2,1,0:T(2,128)(2,1)} %get-tuple-element.15.echo_ref) | copy-start | bytes 294916
  9.5 0.7 %copy-start.2 = (bf16[2,2048]{1,0:T(2,128)(2,1)S(1)}, bf16[2,2048]{1,0:T(2,128)(2,1)}, u32[]{:S(2)}) copy-start(bf16[2,2048]{1,0:T(2,128)(2,1)} %get-tuple-element.16.chirp_ref) | copy-start | bytes 24580
  13.0 5.2 %collective-permute-start.8 = (bf16[16,1024]{1,0:T(8,128)(2,1)S(1)}, bf16[16,1024]{1,0:T(8,128)(2,1)S(1)}, u32[]{:S(2)}, u32[]{:S(2)}) collective-permute-start(bf16[16,1024]{1,0:T(8,128)(2,1)S(1)} %get-tuple-element.21), channel_id=1, source_target_pairs={{0,28},{4,24},{8,20},{12,16},{16,12},{20,8},{24,4},{28,0},{1,29},{... | collective-permute-start | bytes 98312 | tf_op jit(solution)/shard_map/ppermute | solution.py:358
  13.5 5.9 %collective-permute-start.4 = (bf16[16,1024]{1,0:T(8,128)(2,1)S(1)}, bf16[16,1024]{1,0:T(8,128)(2,1)S(1)}, u32[]{:S(2)}, u32[]{:S(2)}) collective-permute-start(bf16[16,1024]{1,0:T(8,128)(2,1)S(1)} %get-tuple-element.21), channel_id=1, source_target_pairs={{0,24},{8,16},{16,8},{24,0},{1,25},{9,17},{17,9},{25,1},{2,26},{10... | collective-permute-start | bytes 98312 | tf_op jit(solution)/shard_map/ppermute | solution.py:350
  15.8 6.0 %collective-permute-start.7 = (bf16[16,1024]{1,0:T(8,128)(2,1)S(1)}, bf16[16,1024]{1,0:T(8,128)(2,1)S(1)}, u32[]{:S(2)}, u32[]{:S(2)}) collective-permute-start(bf16[16,1024]{1,0:T(8,128)(2,1)S(1)} %get-tuple-element.22), channel_id=1, source_target_pairs={{0,20},{4,16},{8,28},{12,24},{16,4},{20,0},{24,12},{28,8},{1,21},{... | collective-permute-start | bytes 98312 | tf_op jit(solution)/shard_map/ppermute | solution.py:358
  17.2 4.5 %collective-permute-start.3 = (bf16[16,1024]{1,0:T(8,128)(2,1)S(1)}, bf16[16,1024]{1,0:T(8,128)(2,1)S(1)}, u32[]{:S(2)}, u32[]{:S(2)}) collective-permute-start(bf16[16,1024]{1,0:T(8,128)(2,1)S(1)} %get-tuple-element.22), channel_id=1, source_target_pairs={{0,16},{8,24},{16,0},{24,8},{1,17},{9,25},{17,1},{25,9},{2,18},{10... | collective-permute-start | bytes 98312 | tf_op jit(solution)/shard_map/ppermute | solution.py:350
  17.8 4.0 %collective-permute-start.6 = (bf16[16,1024]{1,0:T(8,128)(2,1)S(1)}, bf16[16,1024]{1,0:T(8,128)(2,1)S(1)}, u32[]{:S(2)}, u32[]{:S(2)}) collective-permute-start(bf16[16,1024]{1,0:T(8,128)(2,1)S(1)} %get-tuple-element.23), channel_id=1, source_target_pairs={{0,12},{4,8},{8,4},{12,0},{16,28},{20,24},{24,20},{28,16},{1,13},{... | collective-permute-start | bytes 98312 | tf_op jit(solution)/shard_map/ppermute | solution.py:358
  18.2 3.6 %collective-permute-start.2 = (bf16[16,1024]{1,0:T(8,128)(2,1)S(1)}, bf16[16,1024]{1,0:T(8,128)(2,1)S(1)}, u32[]{:S(2)}, u32[]{:S(2)}) collective-permute-start(bf16[16,1024]{1,0:T(8,128)(2,1)S(1)} %get-tuple-element.23), channel_id=1, source_target_pairs={{0,8},{8,0},{16,24},{24,16},{1,9},{9,1},{17,25},{25,17},{2,10},{10... | collective-permute-start | bytes 98312 | tf_op jit(solution)/shard_map/ppermute | solution.py:350
  19.4 3.9 %collective-permute-start.5 = (bf16[16,1024]{1,0:T(8,128)(2,1)S(1)}, bf16[16,1024]{1,0:T(8,128)(2,1)S(1)}, u32[]{:S(2)}, u32[]{:S(2)}) collective-permute-start(bf16[16,1024]{1,0:T(8,128)(2,1)S(1)} %get-tuple-element.24.refs_0_), channel_id=1, source_target_pairs={{0,4},{4,0},{8,12},{12,8},{16,20},{20,16},{24,28},{28,24},{1,5},{5... | collective-permute-start | bytes 98312 | tf_op jit(solution)/shard_map/ppermute | solution.py:358
where the time goes:
time: 24.6 us; the launch traced here: 24.4 us
  starting transfers between devices  13.5 us (55%)
  Pallas kernels  6.9 us (28%)
  waiting for transfers between devices  2.19 us (9%)
  local copies, waits for them, and re-layouts  1.61 us (7%)
    ppermute x4, starting transfers between devices, swap(): return lax.ppermute(value, axis, [(i, i ^ by) for i in range(count)])  5.56 us
    ppermute x1, starting transfers between devices, from_next(): lax.ppermute(value, axis, [(i, (i - 1) % count) for i in range(count)])  5.05 us
    ppermute x4, starting transfers between devices, swap_both(): return lax.ppermute(value, ('section', 'sub'), pairs)  2.9 us
    pallas_call x1, Pallas kernels, prepare(): pl.pallas_call(functools.partial(prepare_kernel, sections=sections, group...  1.98 us
    pallas_call x1, Pallas kernels, fold_operator(): pl.pallas_call(functools.partial(operator_kernel, dims=dims, sections=sec...  1.82 us
    unnamed x6, local copies, waits for them, and re-layouts  1.59 us
    ppermute x4, waiting for transfers between devices, swap_both(): return lax.ppermute(value, ('section', 'sub'), pairs)  1.54 us
    pallas_call x1, Pallas kernels, form_image(): pl.pallas_call(image_kernel, out_shape=jax.ShapeDtypeStruct((height, widt...  1.06 us
  transfers between devices with their start and end apart: 9, of which 2 were waited for; matrix products, arithmetic and copies ran while one was open for 0% of the time, Pallas kernels for 20%

commit v1 on v0

--- a/solution.py
+++ b/solution.py
@@ -17,18 +17,7 @@
     return -(-value // unit) * unit
 
 
-def prepare_kernel(*refs, sections, group):
-    sources, (echo_out, chirp_out, pack_ref), scratch = refs[:7], refs[7:10], refs[10:]
-    coef_ref, start_ref, width_ref, steer_ref, order_ref, starts, sems = scratch
-    targets = (coef_ref, start_ref, width_ref, steer_ref, order_ref, chirp_out, echo_out)
-    loads = [
-        pltpu.make_async_copy(source, target, sems.at[i])
-        for i, (source, target) in enumerate(zip(sources, targets))
-    ]
-    for load in loads:
-        load.start()
-    for load in loads:
-        load.wait()
+def pack_kernel(coef_ref, start_ref, width_ref, steer_ref, order_ref, pack_ref, starts, *, sections, group):
     levels, _, sides, parts, taps, beams = coef_ref.shape
     tap = lax.broadcasted_iota(jnp.int32, (taps, beams), 0)
     row = 0
@@ -66,21 +55,14 @@
     return levels * sides * parts * taps + parts * sections * group + ceil_to(levels * sides, 16)
 
 
-def prepare(echo, chirp, coef, start, width, steer, order, sections, group):
+def pack_parameters(coef, start, width, steer, order, sections, group):
     levels, _, sides, parts, taps, beams = coef.shape
-    sources = (coef, start, width, steer, order, chirp, echo)
     return pl.pallas_call(
-        functools.partial(prepare_kernel, sections=sections, group=group),
-        out_shape=(
-            jax.ShapeDtypeStruct(echo.shape, BF16),
-            jax.ShapeDtypeStruct(chirp.shape, BF16),
-            jax.ShapeDtypeStruct((pack_rows(levels, sides, parts, taps, sections, group), beams), BF16),
-        ),
-        in_specs=[pl.BlockSpec(memory_space=pl.ANY)] * len(sources),
-        scratch_shapes=[pltpu.VMEM(x.shape, x.dtype) for x in sources[:5]]
-        + [pltpu.VMEM((ceil_to(levels * sides, 16), beams), F32), pltpu.SemaphoreType.DMA((len(sources),))],
-        name="prepare",
-    )(*sources)
+        functools.partial(pack_kernel, sections=sections, group=group),
+        out_shape=jax.ShapeDtypeStruct((pack_rows(levels, sides, parts, taps, sections, group), beams), BF16),
+        scratch_shapes=[pltpu.VMEM((ceil_to(levels * sides, 16), beams), F32)],
+        name="pack_parameters",
+    )(coef, start, width, steer, order)
 
 
 def split_two(value):
@@ -251,8 +233,10 @@
         out_ref[s] = as_chunk(done, s, out_ref.shape[2] // LANE, group)
 
 
-def finish_kernel(index_ref, early_ref, late_ref, halo_ref, table, out_ref, rows, even, odd, *, group):
-    section, has_next = index_ref[0], index_ref[1] != 0
+def finish_kernel(
+    index_ref, early_ref, late_ref, halo_ref, halo_odd_ref, table, out_ref, rows, even, odd, *, group
+):
+    section, is_odd, has_next = index_ref[0], index_ref[1] != 0, index_ref[2] != 0
     pulses = halo_ref.shape[0]
     span = late_ref.shape[1]
     extra = even.shape[0] // group - span // LANE
@@ -261,6 +245,7 @@
     rows[:, span:] = jnp.zeros((2 * group, taps), F32)
     for p in range(pulses):
         far = halo_ref[p, :, :taps].astype(F32)
+        far = jnp.where(is_odd, halo_odd_ref[p, :, :taps].astype(F32), far)
         far = jnp.where(has_next, far, 0.0)
         for c in range(2):
             rows[c * group + p : c * group + p + 1, span:] = far[c : c + 1]
@@ -299,17 +284,17 @@
     )(echo, chirp)
 
 
-def finish_compression(index, early, late, halo, table, sections, group):
+def finish_compression(index, early, late, halos, table, sections, group):
     _, height, chunk = early.shape
     blocks = late.shape[1] // LANE + table.shape[0] // (2 * LANE) - 1
     return pl.pallas_call(
         functools.partial(finish_kernel, group=group),
         out_shape=jax.ShapeDtypeStruct((sections, height, chunk), BF16),
-        in_specs=[pl.BlockSpec(memory_space=pltpu.SMEM)] + [pl.BlockSpec(memory_space=pltpu.VMEM)] * 4,
+        in_specs=[pl.BlockSpec(memory_space=pltpu.SMEM)] + [pl.BlockSpec(memory_space=pltpu.VMEM)] * 5,
         scratch_shapes=row_scratch(blocks, group),
         compiler_params=pltpu.CompilerParams(vmem_limit_bytes=24 * 1024 * 1024),
         name="finish_compression",
-    )(index, early, late, halo, table)
+    )(index, early, late, *halos, table)
 
 
 def image_kernel(operator_ref, *refs):
@@ -360,7 +345,11 @@
 
 def from_next(value, axis):
     count = lax.axis_size(axis)
-    return lax.ppermute(value, axis, [(i, (i - 1) % count) for i in range(count)])
+    results = []
+    for parity in range(2):
+        peers = [min(max(((i + parity) ^ 1) - parity, 0), count - 1) for i in range(count)]
+        results.append(lax.ppermute(value, axis, list(enumerate(peers))))
+    return results
 
 
 def on_device(echoes, chirp, steer, pulse_order, band_coef, band_start, band_width):
@@ -373,17 +362,15 @@
     dims = (levels, sides, parts, taps, beams)
 
     section = lax.axis_index("section").astype(jnp.int32)
-    has_next = (lax.axis_index("rng") < lax.axis_size("rng") - 1).astype(jnp.int32)
-    index = jnp.stack([section, has_next])
+    place, last = lax.axis_index("rng").astype(jnp.int32), lax.axis_size("rng") - 1
+    index = jnp.stack([section, place & 1, (place < last).astype(jnp.int32)])
     echo = jnp.transpose(echoes[:, 0], (1, 0, 2))
-    halo = from_next(echo, "rng")
-    echo, chirp, packed = prepare(
-        echo, chirp, coef, band_start, band_width, weights, pulse_order, sections, group
-    )
+    halos = from_next(echo, "rng")
+    packed = pack_parameters(coef, band_start, band_width, weights, pulse_order, sections, group)
     packed_partner = swap(packed, "sub", 1) if subs == 2 else packed
     early, late, table = begin_compression(echo, chirp, sections, group)
-    halo, packed_partner = lax.optimization_barrier((halo, packed_partner))
-    compressed = finish_compression(index, early, late, halo, table, sections, group)
+    *halos, packed_partner = lax.optimization_barrier((*halos, packed_partner))
+    compressed = finish_compression(index, early, late, halos, table, sections, group)
     chunks = [compressed[0]] + [swap(compressed[j], "section", j) for j in range(1, sections)]
     if subs != 2:
         return merge_images(section, chunks, packed, dims, sections, group)

time: 24.6 us -> 25.9 us (1.053)
  starting transfers between devices: 13.5 us -> 15 us
    ppermute x1 -> x2, starting transfers between devices: 5.05 us -> 6.57 us  [from_next(): results.append(lax.ppermute(value, axis, list(enumerate(peers))))]
    ppermute x4, starting transfers between devices: 2.9 us -> 2.61 us  [swap_both(): return lax.ppermute(value, ('section', 'sub'), pairs)]
  transfers between devices with their start and end apart: 9 -> 10, of which waited for: 2 -> 2; matrix products, arithmetic and copies ran while one was open for 0% -> 0% of each run, Pallas kernels for 20% -> 18%
where the time goes in v1:
time: 25.9 us; the launch traced here: 25.7 us
  starting transfers between devices  15 us (58%)
  Pallas kernels  6.73 us (26%)
  waiting for transfers between devices  2.19 us (8%)
  local copies, waits for them, and re-layouts  1.6 us (6%)
    ppermute x2, starting transfers between devices, from_next(): results.append(lax.ppermute(value, axis, list(enumerate(peers))))  6.57 us
    ppermute x4, starting transfers between devices, swap(): return lax.ppermute(value, axis, [(i, i ^ by) for i in range(count)])  5.79 us
    ppermute x4, starting transfers between devices, swap_both(): return lax.ppermute(value, ('section', 'sub'), pairs)  2.61 us
    pallas_call x1, Pallas kernels, fold_operator(): pl.pallas_call(functools.partial(operator_kernel, dims=dims, sections=sec...  1.82 us
    pallas_call x1, Pallas kernels, pack_parameters(): pl.pallas_call(functools.partial(pack_kernel, sections=sections, group=gr...  1.82 us
    unnamed x6, local copies, waits for them, and re-layouts  1.59 us
    ppermute x4, waiting for transfers between devices, swap_both(): return lax.ppermute(value, ('section', 'sub'), pairs)  1.54 us
    pallas_call x1, Pallas kernels, form_image(): pl.pallas_call(image_kernel, out_shape=jax.ShapeDtypeStruct((height, widt...  1.05 us
  transfers between devices with their start and end apart: 10, of which 2 were waited for; matrix products, arithmetic and copies ran while one was open for 0% of the time, Pallas kernels for 18%

profile of v1, /device:TPU:0, one launch (start us, length us, event | category | flops | bytes accessed | tf_op | source)
XLA Modules:
  0.0 25.7 jit_solution(12360334471960281932)
XLA Ops:
  0.0 1.5 %collective-permute-start.1 = (bf16[6,2,4096]{2,1,0:T(2,128)(2,1)}, bf16[6,2,4096]{2,1,0:T(2,128)(2,1)S(1)}, u32[]{:S(2)}, u32[]{:S(2)}) collective-permute-start(bf16[6,2,4096]{2,1,0:T(2,128)(2,1)} %bitcast.19), channel_id=1, source_target_pairs={{0,0},{1,2},{2,1},{3,3},{4,4},{5,6},{6,5},{7,7},{8,8},{9,10},{10,9... | collective-permute-start | bytes 294920 | tf_op jit(solution)/shard_map/ppermute | solution.py:351
  1.5 5.0 %collective-permute-start = (bf16[6,2,4096]{2,1,0:T(2,128)(2,1)}, bf16[6,2,4096]{2,1,0:T(2,128)(2,1)S(1)}, u32[]{:S(2)}, u32[]{:S(2)}) collective-permute-start(bf16[6,2,4096]{2,1,0:T(2,128)(2,1)} %bitcast.20), channel_id=1, source_target_pairs={{0,1},{1,0},{2,3},{3,2},{4,5},{5,4},{6,7},{7,6},{8,9},{9,8},{10,11... | collective-permute-start | bytes 294920 | tf_op jit(solution)/shard_map/ppermute | solution.py:351
  6.6 1.8 %pack_parameters.1.own_ref = bf16[400,128]{1,0:T(8,128)(2,1)} custom-call(bf16[5,1,2,2,16,128]{5,4,3,2,1,0:T(8,128)(2,1)} %bitcast.22, s32[5,1,2,128]{3,2,1,0:T(2,128)} %start_ref.1, s32[5,1,2,128]{3,2,1,0:T(2,128)} %width_ref.1, bf16[2,1,24,128]{3,2,1,0:T(8,128)(2,1)} %bitcast.23, s32[1,24]{1,0:T(1,128)} %order_ref.1), custom_call_target="tpu_custom_call" | custom-call | tf_op jit(solution)/shard_map/pack_parameters/pallas_call | solution.py:60
  8.4 0.0 copy-start
  8.4 1.5 %collective-permute-start.2 = (bf16[400,128]{1,0:T(8,128)(2,1)}, bf16[400,128]{1,0:T(8,128)(2,1)S(1)}, u32[]{:S(2)}, u32[]{:S(2)}) collective-permute-start(bf16[400,128]{1,0:T(8,128)(2,1)} %pack_parameters.1.own_ref), channel_id=1, source_target_pairs={{0,4},{4,0},{1,5},{5,1},{2,6},{6,2},{3,7},{7,3},{8,12},{12,8},{9,1... | collective-permute-start | bytes 307208 | tf_op jit(solution)/shard_map/ppermute | solution.py:335
  9.9 0.0 copy-start.1
  9.9 0.9 %copy-done.1 = bf16[2,1,6,4096]{3,0,2,1:T(2,128)(2,1)S(1)} copy-done((bf16[2,1,6,4096]{3,0,2,1:T(2,128)(2,1)S(1)}, bf16[2,1,6,4096]{3,0,2,1:T(2,128)(2,1)}, u32[]{:S(2)}) %copy-start.1) | copy-done | bytes 98328
  10.8 0.0 copy-start.2
  10.8 0.7 %copy-done.2 = bf16[2,2048]{1,0:T(2,128)(2,1)S(1)} copy-done((bf16[2,2048]{1,0:T(2,128)(2,1)S(1)}, bf16[2,2048]{1,0:T(2,128)(2,1)}, u32[]{:S(2)}) %copy-start.2) | copy-done | bytes 8216
  11.5 1.0 %begin_compression.1 = (bf16[2,16,1024]{2,1,0:T(8,128)(2,1)S(1)}, f32[16,2048]{1,0:T(8,128)S(1)}, bf16[4352,256]{1,0:T(8,128)(2,1)S(1)}) custom-call(bf16[6,2,4096]{2,1,0:T(2,128)(2,1)S(1)} %bitcast.21, bf16[2,2048]{1,0:T(2,128)(2,1)S(1)} %copy-done.2), custom_call_target="tpu_custom_call" | custom-call | tf_op jit(solution)/shard_map/begin_compression/pallas_call | solution.py:274
  12.5 0.1 pad_add_fusion.index_ref
  12.6 0.0 collective-permute-done.1.halo_odd_ref
  12.6 0.0 collective-permute-done.halo_ref
  12.6 0.6 %collective-permute-done.2.partner_ref = bf16[400,128]{1,0:T(8,128)(2,1)S(1)} collective-permute-done((bf16[400,128]{1,0:T(8,128)(2,1)}, bf16[400,128]{1,0:T(8,128)(2,1)S(1)}, u32[]{:S(2)}, u32[]{:S(2)}) %collective-permute-start.2) | collective-permute-done | bytes 102432 | tf_op jit(solution)/shard_map/ppermute | solution.py:335
  13.3 1.0 %finish_compression.1 = bf16[4,16,1024]{2,1,0:T(8,128)(2,1)S(1)} custom-call(s32[3]{0:T(128)S(1)} %pad_add_fusion.index_ref, bf16[2,16,1024]{2,1,0:T(8,128)(2,1)S(1)} %get-tuple-element.12.early_ref, f32[16,2048]{1,0:T(8,128)S(1)} %get-tuple-element.13.late_ref, bf16[6,2,4096]{2,1,0:T(2,128)(2,1)S(1)} %collective-permute-done.halo_ref, ...), custom_call_target="tpu_custom_call" | custom-call | tf_op jit(solution)/shard_map/finish_compression/pallas_call | solution.py:290
  14.3 0.2 collective-permute-start.9
  14.5 2.5 %collective-permute-start.5 = (bf16[16,1024]{1,0:T(8,128)(2,1)S(1)}, bf16[16,1024]{1,0:T(8,128)(2,1)S(1)}, u32[]{:S(2)}, u32[]{:S(2)}) collective-permute-start(bf16[16,1024]{1,0:T(8,128)(2,1)S(1)} %get-tuple-element.17), channel_id=1, source_target_pairs={{0,24},{8,16},{16,8},{24,0},{1,25},{9,17},{17,9},{25,1},{2,26},{10... | collective-permute-start | bytes 98312 | tf_op jit(solution)/shard_map/ppermute | solution.py:335
  17.1 1.4 %collective-permute-start.8 = (bf16[16,1024]{1,0:T(8,128)(2,1)S(1)}, bf16[16,1024]{1,0:T(8,128)(2,1)S(1)}, u32[]{:S(2)}, u32[]{:S(2)}) collective-permute-start(bf16[16,1024]{1,0:T(8,128)(2,1)S(1)} %get-tuple-element.18), channel_id=1, source_target_pairs={{0,20},{4,16},{8,28},{12,24},{16,4},{20,0},{24,12},{28,8},{1,21},{... | collective-permute-start | bytes 98312 | tf_op jit(solution)/shard_map/ppermute | solution.py:343
  18.5 0.5 %collective-permute-start.4 = (bf16[16,1024]{1,0:T(8,128)(2,1)S(1)}, bf16[16,1024]{1,0:T(8,128)(2,1)S(1)}, u32[]{:S(2)}, u32[]{:S(2)}) collective-permute-start(bf16[16,1024]{1,0:T(8,128)(2,1)S(1)} %get-tuple-element.18), channel_id=1, source_target_pairs={{0,16},{8,24},{16,0},{24,8},{1,17},{9,25},{17,1},{25,9},{2,18},{10... | collective-permute-start | bytes 98312 | tf_op jit(solution)/shard_map/ppermute | solution.py:335
  19.0 0.4 %collective-permute-start.7 = (bf16[16,1024]{1,0:T(8,128)(2,1)S(1)}, bf16[16,1024]{1,0:T(8,128)(2,1)S(1)}, u32[]{:S(2)}, u32[]{:S(2)}) collective-permute-start(bf16[16,1024]{1,0:T(8,128)(2,1)S(1)} %get-tuple-element.19), channel_id=1, source_target_pairs={{0,12},{4,8},{8,4},{12,0},{16,28},{20,24},{24,20},{28,16},{1,13},{... | collective-permute-start | bytes 98312 | tf_op jit(solution)/shard_map/ppermute | solution.py:343
  19.5 0.0 collective-permute-done.9.refs_7_
  19.5 1.2 %collective-permute-start.3 = (bf16[16,1024]{1,0:T(8,128)(2,1)S(1)}, bf16[16,1024]{1,0:T(8,128)(2,1)S(1)}, u32[]{:S(2)}, u32[]{:S(2)}) collective-permute-start(bf16[16,1024]{1,0:T(8,128)(2,1)S(1)} %get-tuple-element.19), channel_id=1, source_target_pairs={{0,8},{8,0},{16,24},{24,16},{1,9},{9,1},{17,25},{25,17},{2,10},{10... | collective-permute-start | bytes 98312 | tf_op jit(solution)/shard_map/ppermute | solution.py:335
  20.7 0.0 collective-permute-done.5.refs_3_
  20.7 0.5 %collective-permute-start.6 = (bf16[16,1024]{1,0:T(8,128)(2,1)S(1)}, bf16[16,1024]{1,0:T(8,128)(2,1)S(1)}, u32[]{:S(2)}, u32[]{:S(2)}) collective-permute-start(bf16[16,1024]{1,0:T(8,128)(2,1)S(1)} %get-tuple-element.20.refs_0_), channel_id=1, source_target_pairs={{0,4},{4,0},{8,12},{12,8},{16,20},{20,16},{24,28},{28,24},{1,5},{5... | collective-permute-start | bytes 98312 | tf_op jit(solution)/shard_map/ppermute | solution.py:343
  21.2 0.0 copy-done
  21.2 1.8 %fold_operator.1.operator_ref = bf16[256,256]{1,0:T(8,128)(2,1)S(1)} custom-call(s32[3]{0:T(128)S(1)} %pad_add_fusion.index_ref, bf16[400,128]{1,0:T(8,128)(2,1)S(1)} %copy-done, bf16[400,128]{1,0:T(8,128)(2,1)S(1)} %collective-permute-done.2.partner_ref), custom_call_target="tpu_custom_call" | custom-call | tf_op jit(solution)/shard_map/fold_operator/pallas_call | solution.py:148
  23.0 0.0 collective-permute-done.8.refs_6_
  23.0 0.0 collective-permute-done.4.refs_2_
  23.0 0.0 collective-permute-done.7.refs_5_
  23.1 0.0 collective-permute-done.3.refs_1_
  23.1 1.5 %collective-permute-done.6.refs_4_ = bf16[16,1024]{1,0:T(8,128)(2,1)S(1)} collective-permute-done((bf16[16,1024]{1,0:T(8,128)(2,1)S(1)}, bf16[16,1024]{1,0:T(8,128)(2,1)S(1)}, u32[]{:S(2)}, u32[]{:S(2)}) %collective-permute-start.6) | collective-permute-done | bytes 32800 | tf_op jit(solution)/shard_map/ppermute | solution.py:343
  24.6 1.1 %form_image.1 = bf16[256,1024]{1,0:T(8,128)(2,1)} custom-call(bf16[256,256]{1,0:T(8,128)(2,1)S(1)} %fold_operator.1.operator_ref, bf16[16,1024]{1,0:T(8,128)(2,1)S(1)} %get-tuple-element.20.refs_0_, bf16[16,1024]{1,0:T(8,128)(2,1)S(1)} %collective-permute-done.3.refs_1_, bf16[16,1024]{1,0:T(8,128)(2,1)S(1)} %collective-permute-done.4.refs_2_, ...), custom_call_target="tpu_custom_call" | custom-call | tf_op jit(solution)/shard_map/form_image/pallas_call | solution.py:319
  (1 shorter events, 0.0 us)
Async XLA Ops:
  0.0 12.6 %collective-permute-start.1 = (bf16[6,2,4096]{2,1,0:T(2,128)(2,1)}, bf16[6,2,4096]{2,1,0:T(2,128)(2,1)S(1)}, u32[]{:S(2)}, u32[]{:S(2)}) collective-permute-start(bf16[6,2,4096]{2,1,0:T(2,128)(2,1)} %bitcast.19), channel_id=1, source_target_pairs={{0,0},{1,2},{2,1},{3,3},{4,4},{5,6},{6,5},{7,7},{8,8},{9,10},{10,9... | collective-permute-start | bytes 294920 | tf_op jit(solution)/shard_map/ppermute | solution.py:351
  1.5 11.1 %collective-permute-start = (bf16[6,2,4096]{2,1,0:T(2,128)(2,1)}, bf16[6,2,4096]{2,1,0:T(2,128)(2,1)S(1)}, u32[]{:S(2)}, u32[]{:S(2)}) collective-permute-start(bf16[6,2,4096]{2,1,0:T(2,128)(2,1)} %bitcast.20), channel_id=1, source_target_pairs={{0,1},{1,0},{2,3},{3,2},{4,5},{5,4},{6,7},{7,6},{8,9},{9,8},{10,11... | collective-permute-start | bytes 294920 | tf_op jit(solution)/shard_map/ppermute | solution.py:351
  8.4 12.8 %copy-start = (bf16[400,128]{1,0:T(8,128)(2,1)S(1)}, bf16[400,128]{1,0:T(8,128)(2,1)}, u32[]{:S(2)}) copy-start(bf16[400,128]{1,0:T(8,128)(2,1)} %pack_parameters.1.own_ref) | copy-start | bytes 307204
  8.4 4.9 %collective-permute-start.2 = (bf16[400,128]{1,0:T(8,128)(2,1)}, bf16[400,128]{1,0:T(8,128)(2,1)S(1)}, u32[]{:S(2)}, u32[]{:S(2)}) collective-permute-start(bf16[400,128]{1,0:T(8,128)(2,1)} %pack_parameters.1.own_ref), channel_id=1, source_target_pairs={{0,4},{4,0},{1,5},{5,1},{2,6},{6,2},{3,7},{7,3},{8,12},{12,8},{9,1... | collective-permute-start | bytes 307208 | tf_op jit(solution)/shard_map/ppermute | solution.py:335
  9.9 0.9 %copy-start.1 = (bf16[2,1,6,4096]{3,0,2,1:T(2,128)(2,1)S(1)}, bf16[2,1,6,4096]{3,0,2,1:T(2,128)(2,1)}, u32[]{:S(2)}) copy-start(bf16[2,1,6,4096]{3,0,2,1:T(2,128)(2,1)} %param.7) | copy-start | bytes 294916
  10.8 0.7 %copy-start.2 = (bf16[2,2048]{1,0:T(2,128)(2,1)S(1)}, bf16[2,2048]{1,0:T(2,128)(2,1)}, u32[]{:S(2)}) copy-start(bf16[2,2048]{1,0:T(2,128)(2,1)} %chirp_ref.1) | copy-start | bytes 24580
  14.3 5.2 %collective-permute-start.9 = (bf16[16,1024]{1,0:T(8,128)(2,1)S(1)}, bf16[16,1024]{1,0:T(8,128)(2,1)S(1)}, u32[]{:S(2)}, u32[]{:S(2)}) collective-permute-start(bf16[16,1024]{1,0:T(8,128)(2,1)S(1)} %get-tuple-element.17), channel_id=1, source_target_pairs={{0,28},{4,24},{8,20},{12,16},{16,12},{20,8},{24,4},{28,0},{1,29},{... | collective-permute-start | bytes 98312 | tf_op jit(solution)/shard_map/ppermute | solution.py:343
  14.5 6.1 %collective-permute-start.5 = (bf16[16,1024]{1,0:T(8,128)(2,1)S(1)}, bf16[16,1024]{1,0:T(8,128)(2,1)S(1)}, u32[]{:S(2)}, u32[]{:S(2)}) collective-permute-start(bf16[16,1024]{1,0:T(8,128)(2,1)S(1)} %get-tuple-element.17), channel_id=1, source_target_pairs={{0,24},{8,16},{16,8},{24,0},{1,25},{9,17},{17,9},{25,1},{2,26},{10... | collective-permute-start | bytes 98312 | tf_op jit(solution)/shard_map/ppermute | solution.py:335
  17.1 6.0 %collective-permute-start.8 = (bf16[16,1024]{1,0:T(8,128)(2,1)S(1)}, bf16[16,1024]{1,0:T(8,128)(2,1)S(1)}, u32[]{:S(2)}, u32[]{:S(2)}) collective-permute-start(bf16[16,1024]{1,0:T(8,128)(2,1)S(1)} %get-tuple-element.18), channel_id=1, source_target_pairs={{0,20},{4,16},{8,28},{12,24},{16,4},{20,0},{24,12},{28,8},{1,21},{... | collective-permute-start | bytes 98312 | tf_op jit(solution)/shard_map/ppermute | solution.py:343
  18.5 4.5 %collective-permute-start.4 = (bf16[16,1024]{1,0:T(8,128)(2,1)S(1)}, bf16[16,1024]{1,0:T(8,128)(2,1)S(1)}, u32[]{:S(2)}, u32[]{:S(2)}) collective-permute-start(bf16[16,1024]{1,0:T(8,128)(2,1)S(1)} %get-tuple-element.18), channel_id=1, source_target_pairs={{0,16},{8,24},{16,0},{24,8},{1,17},{9,25},{17,1},{25,9},{2,18},{10... | collective-permute-start | bytes 98312 | tf_op jit(solution)/shard_map/ppermute | solution.py:335
  19.0 4.0 %collective-permute-start.7 = (bf16[16,1024]{1,0:T(8,128)(2,1)S(1)}, bf16[16,1024]{1,0:T(8,128)(2,1)S(1)}, u32[]{:S(2)}, u32[]{:S(2)}) collective-permute-start(bf16[16,1024]{1,0:T(8,128)(2,1)S(1)} %get-tuple-element.19), channel_id=1, source_target_pairs={{0,12},{4,8},{8,4},{12,0},{16,28},{20,24},{24,20},{28,16},{1,13},{... | collective-permute-start | bytes 98312 | tf_op jit(solution)/shard_map/ppermute | solution.py:343
  19.5 3.6 %collective-permute-start.3 = (bf16[16,1024]{1,0:T(8,128)(2,1)S(1)}, bf16[16,1024]{1,0:T(8,128)(2,1)S(1)}, u32[]{:S(2)}, u32[]{:S(2)}) collective-permute-start(bf16[16,1024]{1,0:T(8,128)(2,1)S(1)} %get-tuple-element.19), channel_id=1, source_target_pairs={{0,8},{8,0},{16,24},{24,16},{1,9},{9,1},{17,25},{25,17},{2,10},{10... | collective-permute-start | bytes 98312 | tf_op jit(solution)/shard_map/ppermute | solution.py:335
  20.7 3.9 %collective-permute-start.6 = (bf16[16,1024]{1,0:T(8,128)(2,1)S(1)}, bf16[16,1024]{1,0:T(8,128)(2,1)S(1)}, u32[]{:S(2)}, u32[]{:S(2)}) collective-permute-start(bf16[16,1024]{1,0:T(8,128)(2,1)S(1)} %get-tuple-element.20.refs_0_), channel_id=1, source_target_pairs={{0,4},{4,0},{8,12},{12,8},{16,20},{20,16},{24,28},{28,24},{1,5},{5... | collective-permute-start | bytes 98312 | tf_op jit(solution)/shard_map/ppermute | solution.py:343
